TPU v7x, 32 devices: a whole 2x2x4 slice. The times are simulated.
32 devices in a mesh: grp: 4 (over z), mem: 8 (over y, x, core).
Axes of the slice: x: 2, y: 2, z: 4, core: 2. Of those that a mesh axis runs over, the one named last changes fastest.
Arguments:
- spectra: bfloat16 [128, 8, 2, 1024], P(('grp', 'mem')), may hold values from -6 to 6
- seg_mask: int32 [128, 8], P(('grp', 'mem')), may hold values 0 or 1
- chan_pos: int32 [128], P(('grp', 'mem')), may hold values from 0 to 127, each once
Outputs:
- correlations: bfloat16 [128, 4, 32, 128], P('grp', None, 'mem')
Inputs may be any that keep to these rules, and one draw needn't show every extreme that they name: `seg_mask`: segment validity is 0 or 1. `chan_pos`: each position appears once.
All inputs are finite; a program needn't handle non-finite values. No bound on the sum of `seg_mask` on one device may be relied on, other than what follows from the above.
Results may differ from a plain program's by a relative error of at most 0.0045.
Values may be sent and summed in bfloat16 or wider, within the bound.
A program may use at most 128 MiB of HBM per device.

v0:
```python
import math

import jax
import jax.numpy as jnp
from jax import lax
from jax.sharding import PartitionSpec as P

BINS = 1024
LAGS = 128


def make_table(bins, lags):
    freq = jnp.arange(bins, dtype=jnp.int32)
    lag_ids = jnp.arange(lags, dtype=jnp.int32) - lags // 2
    phase = jnp.mod(freq[:, None] * lag_ids[None, :], bins).astype(jnp.float32) * (
        2.0 * math.pi / bins
    )
    table = jnp.concatenate([jnp.cos(phase), -jnp.sin(phase)], axis=0).astype(jnp.bfloat16)
    return (table, lag_ids.astype(jnp.float32))


def pick_block(count, most):
    best = 1
    for candidate in range(1, count + 1):
        if count % candidate == 0 and candidate <= most:
            best = candidate
    return best


def correlate(rows, cols, table, lag_vals, ratio, scale):
    row_spec, row_ints = rows
    col_spec, col_ints = cols
    nrows = row_spec.shape[0]
    ncols = col_spec.shape[0]
    segs = col_spec.shape[1]
    bins = col_spec.shape[3]
    lags = table.shape[1]
    col_flat = col_spec.reshape(ncols, 2 * segs, bins)
    turned = jnp.stack((-col_spec[:, :, 1], col_spec[:, :, 0]), axis=2).reshape(
        ncols, 2 * segs, bins
    )
    bstack = jnp.stack([col_flat, turned], axis=1)
    col_mask = col_ints[:, :segs].astype(jnp.float32)
    col_pos = col_ints[:, segs].astype(jnp.float32)
    block = pick_block(nrows, max(1, 1024 // ncols))

    def one_block(args):
        spec_blk, int_blk = args
        cross = jnp.einsum(
            "itf,jctf->ijcf", spec_blk, bstack, preferred_element_type=jnp.float32
        ).astype(jnp.bfloat16)
        raw = jnp.dot(
            cross.reshape(block * ncols, 2 * bins), table, preferred_element_type=jnp.float32
        ).reshape(block, ncols, lags)
        count = jnp.dot(
            int_blk[:, :segs].astype(jnp.float32), col_mask.T, precision=lax.Precision.HIGHEST
        )
        dist = jnp.abs(int_blk[:, segs].astype(jnp.float32)[:, None] - col_pos[None, :])
        span = 1.0 + dist * ratio
        taper = 1.0 / (1.0 + (lag_vals / span[:, :, None]) ** 2)
        norm = 1.0 / (scale * jnp.maximum(count, 1.0))
        return (raw * taper * norm[:, :, None]).astype(jnp.bfloat16)

    spec_rows = row_spec.reshape(nrows // block, block, 2 * segs, bins)
    int_rows = row_ints.reshape(nrows // block, block, row_ints.shape[1])
    out = lax.map(one_block, (spec_rows, int_rows))
    return out.reshape(nrows, ncols, lags)


def body(spectra, seg_mask, chan_pos):
    masked = spectra * seg_mask.astype(jnp.bfloat16)[:, :, None, None]
    ints = jnp.concatenate([seg_mask, chan_pos[:, None]], axis=1)
    chans = spectra.shape[0] * lax.axis_size("grp") * lax.axis_size("mem")
    table, lag_vals = make_table(BINS, LAGS)
    ratio = LAGS / chans
    scale = math.sqrt(BINS)
    cols = (
        lax.all_gather(masked, "grp", axis=0, tiled=True),
        lax.all_gather(ints, "grp", axis=0, tiled=True),
    )
    result = correlate(
        lax.all_gather((masked, ints), "mem", axis=0, tiled=True),
        cols,
        table,
        lag_vals,
        ratio,
        scale,
    )
    return result.reshape(result.shape[0], lax.axis_size("grp"), spectra.shape[0], LAGS)


def solution(mesh):
    in_specs = (P(("grp", "mem"), None, None, None), P(("grp", "mem"), None), P(("grp", "mem")))
    out_specs = P("grp", None, "mem", None)
    return jax.shard_map(body, mesh=mesh, in_specs=in_specs, out_specs=out_specs, check_vma=False)
```

profile of v0, /device:TPU:0, one launch (start us, length us, event | category | flops | bytes accessed | tf_op | source)
XLA Modules:
  0.0 105.4 jit_solution(3508888565890975375)
XLA Ops:
  6.5 0.0 all-gather.4.cloned.1.call-start
  6.5 0.7 convert_element_type.51
  7.2 1.6 %copy_multiply_fusion = bf16[4,8,2,1024]{3,1,2,0:T(8,128)(2,1)} fusion(bf16[4,8,2,1024]{3,2,1,0:T(2,128)(2,1)} %param.3, bf16[4,8]{1,0:T(4,128)(2,1)S(1)} %convert_element_type.51), kind=kLoop, calls=%fused_computation.30 | loop fusion | flops 65536 | bytes 262208 | tf_op jit(solution)/shard_map/mul | solution.py:71
  8.9 0.0 all-gather.4.cloned.1.call-update
  8.9 17.6 %all_gather.12 = bf16[16,8,2,1024]{3,1,2,0:T(8,128)(2,1)S(1)} all-gather(bf16[4,8,2,1024]{3,1,2,0:T(8,128)(2,1)} %copy_multiply_fusion), channel_id=1, replica_groups=mesh['grp'=4,'mem'=8] {'grp'}, dimensions={0}, use_global_device_ids=true | all-gather | bytes 655360 | tf_op jit(solution)/shard_map/all_gather | solution.py:78
  26.5 0.3 copy.38
  26.8 0.1 pad_maximum_fusion
  26.9 0.0 copy-start.1
  26.9 0.0 copy-start
  26.9 4.9 %copy.42 = bf16[16,1,16,1024]{2,0,1,3:T(8,128)(2,1)} copy(bf16[16,1,16,1024]{3,0,2,1:T(8,128)(2,1)S(1)} %bitcast.24) | data formatting | bytes 1048576 | tf_op jit(solution)/shard_map/stack;reshape | solution.py:42
  31.8 4.9 %copy.41 = bf16[16,1,16,1024]{2,0,1,3:T(8,128)(2,1)} copy(bf16[16,1,16,1024]{3,0,2,1:T(8,128)(2,1)S(1)} %bitcast.22) | data formatting | bytes 1048576 | tf_op jit(solution)/shard_map/stack;reshape | solution.py:42
  36.7 0.0 copy-done.1
  36.7 0.1 copy.45
  36.8 0.0 copy-done
  36.8 0.1 add_bitcast_fusion
  36.9 8.9 %all-gather = s32[8,4,9]{2,1,0:T(4,128)S(1)} all-gather(s32[1,4,9]{2,1,0:T(4,128)S(1)} %add_bitcast_fusion), channel_id=1, replica_groups=mesh['grp'=4,'mem'=8] {'mem'}, dimensions={0}, use_global_device_ids=true | all-gather | bytes 1296 | tf_op jit(solution)/shard_map/all_gather | solution.py:82
  45.8 0.1 slice_convert_fusion.2
  45.8 0.1 copy.53
  45.9 12.2 %all-gather.1 = s32[4,4,9]{2,1,0:T(4,128)S(1)} all-gather(s32[1,4,9]{2,1,0:T(4,128)S(1)} %add_bitcast_fusion), channel_id=1, replica_groups=mesh['grp'=4,'mem'=8] {'grp'}, dimensions={0}, use_global_device_ids=true | all-gather | bytes 720 | tf_op jit(solution)/shard_map/all_gather | solution.py:79
  58.1 0.1 slice_convert_fusion.5
  58.1 0.1 copy.54
  58.2 0.1 abs_add_fusion
  58.3 0.1 copy.48
  58.4 0.2 fusion.9
  58.5 0.1 copy.49
  58.6 2.2 %cosine_convert_fusion = (bf16[1024,128]{1,0:T(8,128)(2,1)S(1)}, bf16[1024,128]{1,0:T(8,128)(2,1)S(1)}) fusion(s32[128]{0:T(128)S(1)} %iota_add_fusion), kind=kLoop, calls=%fused_computation.22 | loop fusion | flops 2228224 | bytes 524800 | tf_op jit(solution)/shard_map/convert
  60.9 0.0 all-gather.4.cloned.1.call-done
  60.9 7.7 %copy.43 = bf16[32,8,2,1024]{0,2,1,3:T(2,128)(2,1)} copy(bf16[32,8,2,1024]{3,1,2,0:T(8,128)(2,1)} %all-gather.4.cloned.1.call-done) | data formatting | bytes 2097152 | tf_op jit(solution)/shard_map/all_gather | solution.py:82
  68.6 10.2 %convert_bitcast_fusion = bf16[32,16,2,1024]{0,1,2,3:T(8,128)(2,1)} fusion(bf16[32,16,1024,1]{0,1,3,2:T(8,128)(2,1)} %bitcast.23, bf16[16,1,16,1024]{2,0,1,3:T(8,128)(2,1)} %copy.42, bf16[16,1,16,1024]{2,0,1,3:T(8,128)(2,1)} %copy.41), kind=kOutput, calls=%fused_computation.4 | convolution fusion | flops 35127296 | bytes 4194304 | tf_op jit(solution)/shard_map/while/body/eval_jaxpr/itf,jctf->ijcf/dot_general | solution.py:49
  78.8 14.0 %copy.44 = bf16[32,16,2,1024]{3,2,1,0:T(2,128)(2,1)S(1)} copy(bf16[32,16,2,1024]{0,1,2,3:T(8,128)(2,1)} %convert_bitcast_fusion) | data formatting | bytes 4194304 | tf_op jit(solution)/shard_map/while/body/eval_jaxpr/convert_element_type | solution.py:51
  92.8 2.8 %dot_general.15 = bf16[32,16,2048]{2,1,0:T(8,128)(2,1)} reshape(bf16[32,16,2,1024]{3,2,1,0:T(2,128)(2,1)S(1)} %copy.44) | data formatting | bytes 4194304 | tf_op jit(solution)/shard_map/while/body/eval_jaxpr/dot_general | solution.py:52
  95.6 3.0 %fusion.7 = bf16[32,16,128]{2,1,0:T(8,128)(2,1)} fusion(bf16[32,16,2048]{2,1,0:T(8,128)(2,1)} %dot_general.15, bf16[1024,128]{1,0:T(8,128)(2,1)S(1)} %get-tuple-element.24, bf16[1024,128]{1,0:T(8,128)(2,1)S(1)} %get-tuple-element.23, f32[32,16]{1,0:T(8,128)S(1)} %copy.49, f32[32,16]{1,0:T(8,128)S(1)} %copy.48, f32[128]{0:T(128)S(1)} %fusion.20), kind=kOutput, calls=%fused_computation.7 | convolution fusion | flops 269942784 | bytes 2757120 | tf_op jit(solution)/shard_map/while/body/eval_jaxpr/dot_general | solution.py:52
  (3 shorter events, 0.0 us)
Async XLA Ops:
  6.5 54.4 %all-gather.4.cloned.1.call-start = ((), (), s32[]{:S(2)}) async-start(), calls=%async_computation | async-start | bytes 1179648 | tf_op jit(solution)/shard_map/all_gather | solution.py:82
  26.9 9.8 %copy-start.1 = (s32[4]{0:T(128)S(1)}, s32[4]{0:T(128)}, u32[]{:S(2)}) copy-start(s32[4]{0:T(128)} %param.5) | copy-start | bytes 52
  26.9 9.9 %copy-start = (s32[4,8]{1,0:T(4,128)S(1)}, s32[4,8]{1,0:T(4,128)}, u32[]{:S(2)}) copy-start(s32[4,8]{1,0:T(4,128)} %param.4) | copy-start | bytes 388
Sparse Core Ops, SparseCore 0:
  9.2 26.1 all-gather.3
where the time goes:
time: 106 us; the launch traced here: 105 us
  blocking collectives  38.6 us (36%)
  local copies, waits for them, and re-layouts  35 us (33%)
  between operations  13.5 us (13%)
  matrix products  13.3 us (13%)
  other arithmetic  4.95 us (5%)
    all_gather x1, blocking collectives, body(): lax.all_gather(masked, 'grp', axis=0, tiled=True)  17.6 us
    convert_element_type x1, local copies, waits for them, and re-layouts, one_block(): cross = jnp.einsum('itf,jctf->ijcf', spec_blk, bstack, preferred_element_...  14 us
    all_gather x1, blocking collectives, body(): lax.all_gather(ints, 'grp', axis=0, tiled=True)  12.2 us
    dot_general x1, matrix products, one_block(): jnp.einsum('itf,jctf->ijcf', spec_blk, bstack, preferred_element_type=jnp...  10.2 us
    another operation x2, local copies, waits for them, and re-layouts, correlate(): bstack = jnp.stack([col_flat, turned], axis=1)  9.81 us
    all_gather x1, blocking collectives, body(): lax.all_gather((masked, ints), 'mem', axis=0, tiled=True)  8.89 us
    all_gather x1, local copies, waits for them, and re-layouts, body(): lax.all_gather((masked, ints), 'mem', axis=0, tiled=True)  7.69 us
    dot_general x1, matrix products, one_block(): jnp.dot(cross.reshape(block * ncols, 2 * bins), table, preferred_element_...  2.96 us
  transfers between devices with their start and end apart: 1, of which 0 were waited for; matrix products, arithmetic and copies ran while one was open for 13% of the time, Pallas kernels for 0%

commit v1 on v0

v1 whole, which is shorter than its diff:
```python
import functools
import math

import jax
import jax.numpy as jnp
import ml_dtypes
import numpy as np
from jax import lax
from jax.experimental import pallas as pl
from jax.experimental.pallas import tpu as pltpu
from jax.sharding import PartitionSpec as P

LAGS = 128
LANES = 128
META = 16
MESH = pl.DeviceIdType.MESH


def make_table(bins, lags):
    freq = np.arange(bins, dtype=np.int64)
    lag_ids = np.arange(lags, dtype=np.int64) - lags // 2
    phase = np.mod(freq[:, None] * lag_ids[None, :], bins) * (2.0 * math.pi / bins)
    table = np.concatenate([np.cos(phase), -np.sin(phase)], axis=0)
    return table.astype(np.float32).astype(ml_dtypes.bfloat16)


def flip(me, other, size):
    out, bit = 0, 1
    while bit < size:
        out = out + bit * ((me // bit + other // bit) % 2)
        bit *= 2
    return out


def kernel(n_grp, n_mem, ch, segs, bins, ratio, scale, x_ref, table_hbm, out_ref,
           rows, cols, turned, meta, cross, table, row_send, row_recv, col_send, col_recv, table_sem):
    g = lax.axis_index("grp")
    m = lax.axis_index("mem")
    sub = bins // LANES
    tile = 2 * sub
    per = segs * tile
    body_rows = ch * per
    ncols = n_grp * ch

    table_copy = pltpu.make_async_copy(table_hbm, table, table_sem)
    table_copy.start()

    barrier = pltpu.get_barrier_semaphore()
    for r in range(1, n_mem):
        pl.semaphore_signal(barrier, inc=1, device_id=(g, flip(m, r, n_mem)), device_id_type=MESH)
    for k in range(1, n_grp):
        pl.semaphore_signal(barrier, inc=1, device_id=((g + k) % n_grp, m), device_id_type=MESH)
    pl.semaphore_wait(barrier, n_mem + n_grp - 2)

    row_copies = [None]
    col_copies = [None]
    for k in range(1, n_grp):
        copy = pltpu.make_async_remote_copy(
            src_ref=x_ref, dst_ref=cols.at[g], send_sem=col_send.at[k], recv_sem=col_recv.at[k],
            device_id=((g + k) % n_grp, m), device_id_type=MESH)
        copy.start()
        col_copies.append(copy)
    for r in range(1, n_mem):
        copy = pltpu.make_async_remote_copy(
            src_ref=x_ref, dst_ref=rows.at[r], send_sem=row_send.at[r], recv_sem=row_recv.at[r],
            device_id=(g, flip(m, r, n_mem)), device_id_type=MESH)
        copy.start()
        row_copies.append(copy)

    def prepare(slot):
        def turn(t, carry):
            x = cols[slot, pl.ds(pl.multiple_of(t * tile, tile), tile), :].astype(jnp.float32)
            y = jnp.concatenate([-x[sub:], x[:sub]], axis=0).astype(jnp.bfloat16)
            turned[slot, pl.ds(pl.multiple_of(t * tile, tile), tile), :] = y
            return carry
        lax.fori_loop(0, ch * segs, turn, 0, unroll=8)

    rows[0] = x_ref[...]
    cols[pl.ds(g, 1)] = x_ref[...][None]
    prepare(g)
    for k in range(1, n_grp):
        col_copies[k].wait_recv()
        prepare((g + n_grp - k) % n_grp)
    for q in range(n_grp):
        meta[q * ch:(q + 1) * ch, :] = cols[q, body_rows:body_rows + META, :].astype(jnp.float32)[:ch]
    table_copy.wait()

    lane = lax.broadcasted_iota(jnp.int32, (1, LANES), 1)
    seg_lane = jnp.where(lane < segs, 1.0, 0.0)
    pos_lane = jnp.where(lane == segs, 128.0, 0.0) + jnp.where(lane == segs + 1, 1.0, 0.0)
    lag = (lax.broadcasted_iota(jnp.int32, (1, LAGS), 1) - LAGS // 2).astype(jnp.float32)
    lag2 = lag * lag

    def total(parts):
        quads = []
        for at in range(0, segs, 4):
            quad = parts[at:at + 4]
            while len(quad) > 1:
                quad = [quad[k] + quad[k + 1] if k + 1 < len(quad) else quad[k]
                        for k in range(0, len(quad), 2)]
            quads.append(quad[0].astype(jnp.float32))
        acc = quads[0]
        for one in quads[1:]:
            acc = acc + one
        return acc[:sub] + acc[sub:]

    def step(r, carry):
        @pl.when(r > 0)
        def _():
            pltpu.make_async_remote_copy(
                src_ref=x_ref, dst_ref=rows.at[r], send_sem=row_send.at[r], recv_sem=row_recv.at[r],
                device_id=(g, flip(m, r, n_mem)), device_id_type=MESH).wait_recv()

        def one_col(j, c2):
            slot = j // ch
            base = (j % ch) * per
            q, t = [], []
            for s in range(segs):
                at = pl.ds(pl.multiple_of(base + s * tile, tile), tile)
                q.append(cols[slot, at, :])
                t.append(turned[slot, at, :])
            for i in range(ch):
                p = [rows[r, i * per + s * tile:i * per + (s + 1) * tile, :] for s in range(segs)]
                at = pl.multiple_of((i * ncols + j) * tile, tile)
                cross[pl.ds(at, sub), :] = total([a * b for a, b in zip(p, q)])
                cross[pl.ds(at + sub, sub), :] = total([a * b for a, b in zip(p, t)])
            return c2

        lax.fori_loop(0, ncols, one_col, 0, unroll=2)
        raw = jnp.zeros((ch * ncols, LAGS), jnp.float32)
        for k in range(0, tile, 2):
            left = jnp.concatenate(
                [cross[pl.ds(k + d, ch * ncols, stride=tile), :].astype(jnp.bfloat16) for d in range(2)], axis=1)
            raw = raw + jnp.dot(left, table[k * LANES:(k + 2) * LANES, :], preferred_element_type=jnp.float32)
        mine = rows[r, body_rows:body_rows + META, :].astype(jnp.float32)
        theirs = meta[...]
        pos_j = jnp.sum(theirs * pos_lane, axis=1, keepdims=True)
        start = flip(m, r, n_mem) * ch
        for i in range(ch):
            one = mine[i:i + 1]
            count = jnp.sum(theirs * (one * seg_lane), axis=1, keepdims=True)
            pos_i = jnp.sum(one * pos_lane, axis=1, keepdims=True)
            span = 1.0 + jnp.abs(pos_i - pos_j) * ratio
            span2 = span * span
            factor = span2 / ((span2 + lag2) * (scale * jnp.maximum(count, 1.0)))
            out_ref[start + i] = (raw[i * ncols:(i + 1) * ncols] * factor).astype(jnp.bfloat16)
        return carry

    lax.fori_loop(0, n_mem, step, 0)

    for copy in row_copies[1:] + col_copies[1:]:
        copy.wait_send()


def body(spectra, seg_mask, chan_pos):
    ch, segs, _, bins = spectra.shape
    n_grp, n_mem = lax.axis_size("grp"), lax.axis_size("mem")
    masked = spectra * seg_mask.astype(jnp.bfloat16)[:, :, None, None]
    flat = masked.reshape(-1, LANES)
    notes = jnp.concatenate(
        [seg_mask, (chan_pos // 128)[:, None], (chan_pos % 128)[:, None]], axis=1).astype(jnp.bfloat16)
    notes = jnp.pad(notes, ((0, META - ch), (0, LANES - segs - 2)))
    message = jnp.concatenate([flat, notes], axis=0)
    size = message.shape[0]
    ncols = n_grp * ch
    out = pl.pallas_call(
        functools.partial(kernel, n_grp, n_mem, ch, segs, bins, LAGS / (ch * n_grp * n_mem), math.sqrt(bins)),
        out_shape=jax.ShapeDtypeStruct((n_mem * ch, ncols, LAGS), jnp.bfloat16),
        in_specs=[pl.BlockSpec(memory_space=pltpu.VMEM), pl.BlockSpec(memory_space=pl.ANY)],
        out_specs=pl.BlockSpec(memory_space=pltpu.VMEM),
        scratch_shapes=[
            pltpu.VMEM((n_mem, size, LANES), jnp.bfloat16),
            pltpu.VMEM((n_grp, size, LANES), jnp.bfloat16),
            pltpu.VMEM((n_grp, size, LANES), jnp.bfloat16),
            pltpu.VMEM((ncols, LANES), jnp.float32),
            pltpu.VMEM((ch * ncols * 2 * (bins // LANES), LANES), jnp.float32),
            pltpu.VMEM((2 * bins, LAGS), jnp.bfloat16),
            pltpu.SemaphoreType.DMA((n_mem,)),
            pltpu.SemaphoreType.DMA((n_mem,)),
            pltpu.SemaphoreType.DMA((n_grp,)),
            pltpu.SemaphoreType.DMA((n_grp,)),
            pltpu.SemaphoreType.DMA,
        ],
        compiler_params=pltpu.CompilerParams(
            collective_id=0, has_side_effects=True, vmem_limit_bytes=48 * 1024 * 1024),
    )(message, jnp.asarray(make_table(bins, LAGS)))
    return out.reshape(n_mem * ch, n_grp, ch, LAGS)


def solution(mesh):
    in_specs = (P(("grp", "mem"), None, None, None), P(("grp", "mem"), None), P(("grp", "mem")))
    out_specs = P("grp", None, "mem", None)
    return jax.shard_map(body, mesh=mesh, in_specs=in_specs, out_specs=out_specs, check_vma=False)
```

time: 106 us -> 29.5 us (0.28)
  blocking collectives: 38.6 us -> 0 us
  local copies, waits for them, and re-layouts: 35 us -> 0.97 us
  Pallas kernels: 0 us -> 25.7 us
  between operations: 13.5 us -> 0.04 us
  matrix products: 13.3 us -> 0 us
  other arithmetic: 4.95 us -> 2.6 us
    all_gather x3 -> x0, blocking collectives: 38.6 us -> none  [the longest x1 17.6 us: body(): lax.all_gather(masked, 'grp', axis=0, tiled=True)]
    pallas_call x0 -> x1, Pallas kernels: none -> 25.7 us  [body(): pl.pallas_call(functools.partial(kernel, n_grp, n_mem, ch, segs, bins, LA...]
    convert_element_type x1 -> x0, local copies, waits for them, and re-layouts: 14 us -> none  [one_block(): cross = jnp.einsum('itf,jctf->ijcf', spec_blk, bstack, preferred_element_...]
    dot_general x3 -> x0, matrix products: 13.3 us -> none  [the longest x1 10.2 us: one_block(): jnp.einsum('itf,jctf->ijcf', spec_blk, bstack, preferred_element_type=jnp...]
    another operation x2 -> x0, local copies, waits for them, and re-layouts: 9.81 us -> none  [correlate(): bstack = jnp.stack([col_flat, turned], axis=1)]
    all_gather x2 -> x0, local copies, waits for them, and re-layouts: 7.98 us -> none  [the longest x1 7.69 us: body(): lax.all_gather((masked, ints), 'mem', axis=0, tiled=True)]
    dot_general x1 -> x0, local copies, waits for them, and re-layouts: 2.8 us -> none  [one_block(): jnp.dot(cross.reshape(block * ncols, 2 * bins), table, preferred_element_...]
    another operation x2 -> x0, other arithmetic: 2.28 us -> none
  transfers between devices with their start and end apart: 1 -> 0, of which waited for: 0 -> 0; matrix products, arithmetic and copies ran while one was open for 13% -> 0% of each run, Pallas kernels for 0% -> 0%
where the time goes in v1:
time: 29.5 us; the launch traced here: 29.3 us
  Pallas kernels  25.7 us (87%)
  other arithmetic  2.6 us (9%)
  local copies, waits for them, and re-layouts  0.97 us (3%)
    pallas_call x1, Pallas kernels, body(): pl.pallas_call(functools.partial(kernel, n_grp, n_mem, ch, segs, bins, LA...  25.7 us
    mul x1, other arithmetic, body(): masked = spectra * seg_mask.astype(jnp.bfloat16)[:, :, None, None]  1.1 us
    convert_element_type x1, other arithmetic, body(): masked = spectra * seg_mask.astype(jnp.bfloat16)[:, :, None, None]  0.74 us
    broadcast_in_dim x1, other arithmetic, body(): (chan_pos // 128)[:, None]  0.67 us
    unnamed x3, local copies, waits for them, and re-layouts  0.66 us

profile of v1, /device:TPU:0, one launch (start us, length us, event | category | flops | bytes accessed | tf_op | source)
XLA Modules:
  0.0 29.3 jit_solution(15311626662119225947)
XLA Ops:
  0.0 0.0 copy-start
  0.0 0.7 %convert_element_type.6 = bf16[4,8]{1,0:T(4,128)(2,1)S(1)} convert(s32[4,8]{1,0:T(4,128)} %param.5) | non-fusion elementwise | flops 32 | bytes 192 | tf_op jit(solution)/shard_map/convert_element_type | solution.py:158
  0.7 0.7 %convert_bitcast_fusion = (bf16[4,1]{0,1:T(2,128)(2,1)S(1)}, bf16[4,1]{0,1:T(2,128)(2,1)S(1)}) fusion(s32[4]{0:T(128)} %param.6), kind=kLoop, calls=%fused_computation.20 | loop fusion | flops 84 | bytes 32 | tf_op jit(solution)/shard_map/broadcast_in_dim | solution.py:161
  1.4 0.1 copy.5
  1.5 0.1 copy.6
  1.6 0.1 fusion.8
  1.7 1.1 %broadcast_multiply_fusion = bf16[4,8,2,1024]{3,2,1,0:T(2,128)(2,1)S(1)} fusion(bf16[4,8,2,1024]{3,2,1,0:T(2,128)(2,1)} %param.4, bf16[4,8]{1,0:T(4,128)(2,1)S(1)} %convert_element_type.6), kind=kLoop, calls=%fused_computation.1 | loop fusion | flops 65536 | bytes 262208 | tf_op jit(solution)/shard_map/mul | solution.py:158
  2.8 0.1 reshape.7
  2.9 0.0 copy-done
  2.9 25.7 %shard_map.46 = bf16[32,16,128]{2,1,0:T(8,128)(2,1)S(1)} custom-call(bf16[528,128]{1,0:T(8,128)(2,1)S(1)} %pad_maximum_fusion.x_ref, bf16[2048,128]{1,0:T(8,128)(2,1)S(1)} %copy-done), custom_call_target="tpu_custom_call" | custom-call | tf_op jit(solution)/shard_map/pallas_call | solution.py:166
  28.6 0.7 %copy.8 = bf16[32,4,4,128]{3,2,1,0:T(4,128)(2,1)} copy(bf16[32,4,4,128]{3,2,1,0:T(4,128)(2,1)S(1)} %bitcast.5) | data formatting | bytes 262144
  (1 shorter events, 0.0 us)
Async XLA Ops:
  0.0 2.9 %copy-start = (bf16[2048,128]{1,0:T(8,128)(2,1)S(1)}, bf16[2048,128]{1,0:T(8,128)(2,1)}, u32[]{:S(2)}) copy-start(bf16[2048,128]{1,0:T(8,128)(2,1)} %constant.33.clone.table_hbm) | copy-start | bytes 1572868

commit v2 on v1

v2 whole, which is shorter than its diff:
```python
import functools
import math

import jax
import jax.numpy as jnp
import ml_dtypes
import numpy as np
from jax import lax
from jax.experimental import pallas as pl
from jax.experimental.pallas import tpu as pltpu
from jax.sharding import PartitionSpec as P

LAGS = 128
LANES = 128
META = 16
MESH = pl.DeviceIdType.MESH


def make_table(bins, lags):
    freq = np.arange(bins, dtype=np.int64)
    lag_ids = np.arange(lags, dtype=np.int64) - lags // 2
    phase = np.mod(freq[:, None] * lag_ids[None, :], bins) * (2.0 * math.pi / bins)
    table = np.concatenate([np.cos(phase), -np.sin(phase)], axis=0)
    return table.astype(np.float32).astype(ml_dtypes.bfloat16)


def flip(me, other, size):
    out, bit = 0, 1
    while bit < size:
        out = out + bit * ((me // bit + other // bit) % 2)
        bit *= 2
    return out


def kernel(n_grp, n_mem, ch, segs, bins, ratio, scale, x_ref, mask_ref, pos_ref, table_hbm, out_ref,
           rows, cols, turned, meta, cross, table, row_send, row_recv, col_send, col_recv, table_sem):
    g = lax.axis_index("grp")
    m = lax.axis_index("mem")
    sub = bins // LANES
    tile = 2 * sub
    per = segs * tile
    body_rows = ch * per
    pairs = n_mem * ch * ch

    barrier = pltpu.get_barrier_semaphore()
    partners = [1] + list(range(2, n_mem, 2))
    for r in partners:
        pl.semaphore_signal(barrier, inc=1, device_id=(g, flip(m, r, n_mem)), device_id_type=MESH)
    for k in range(1, n_grp):
        pl.semaphore_signal(barrier, inc=1, device_id=(flip(g, k, n_grp), m), device_id_type=MESH)

    table_copy = pltpu.make_async_copy(table_hbm, table, table_sem)
    table_copy.start()

    lane = lax.broadcasted_iota(jnp.int32, (1, LANES), 1)

    def turn(slot, t, x):
        y = jnp.concatenate([-x[sub:], x[:sub]], axis=0).astype(jnp.bfloat16)
        turned[slot, pl.ds(pl.multiple_of(t * tile, tile), tile), :] = y

    notes = []
    for c in range(ch):
        place = pos_ref[c]
        note = jnp.where(lane == segs, (place // 128).astype(jnp.float32), 0.0)
        note = jnp.where(lane == segs + 1, (place % 128).astype(jnp.float32), note)
        for s in range(segs):
            valid = mask_ref[c, s].astype(jnp.float32)
            note = jnp.where(lane == s, valid, note)
            t = c * segs + s
            x = x_ref[t * tile:(t + 1) * tile, :].astype(jnp.float32) * valid
            packed = x.astype(jnp.bfloat16)
            rows[0, t * tile:(t + 1) * tile, :] = packed
            cols[0, t * tile:(t + 1) * tile, :] = packed
            turn(0, t, x)
        notes.append(note)
    notes.append(jnp.zeros((META - ch, LANES), jnp.float32))
    rows[0, body_rows:, :] = jnp.concatenate(notes, axis=0).astype(jnp.bfloat16)
    cols[0, body_rows:, :] = jnp.concatenate(notes, axis=0).astype(jnp.bfloat16)

    pl.semaphore_wait(barrier, len(partners) + n_grp - 1)

    def row_copy(r, src, to):
        return pltpu.make_async_remote_copy(
            src_ref=rows.at[src], dst_ref=rows.at[r], send_sem=row_send.at[r], recv_sem=row_recv.at[r],
            device_id=(g, flip(m, to, n_mem)), device_id_type=MESH)

    def col_copy(k):
        return pltpu.make_async_remote_copy(
            src_ref=rows.at[0], dst_ref=cols.at[k], send_sem=col_send.at[k], recv_sem=col_recv.at[k],
            device_id=(flip(g, k, n_grp), m), device_id_type=MESH)

    for k in range(1, n_grp):
        col_copy(k).start()
    for r in partners[1:]:
        row_copy(r, 0, r).start()
    row_copy(1, 0, 1).start()

    pos_lane = jnp.where(lane == segs, 128.0, 0.0) + jnp.where(lane == segs + 1, 1.0, 0.0)
    seg_lane = jnp.where(lane < segs, 1.0, 0.0)
    lag = (lax.broadcasted_iota(jnp.int32, (1, LAGS), 1) - LAGS // 2).astype(jnp.float32)
    lag2 = lag * lag

    def total(parts):
        quads = []
        for at in range(0, segs, 4):
            quad = parts[at:at + 4]
            while len(quad) > 1:
                quad = [quad[k] + quad[k + 1] if k + 1 < len(quad) else quad[k]
                        for k in range(0, len(quad), 2)]
            quads.append(quad[0].astype(jnp.float32))
        acc = quads[0]
        for one in quads[1:]:
            acc = acc + one
        return acc[:sub] + acc[sub:]

    def block(r, k):
        def one_col(j, carry):
            base = j * per
            q, t = [], []
            for s in range(segs):
                at = pl.ds(pl.multiple_of(base + s * tile, tile), tile)
                q.append(cols[k, at, :])
                t.append(turned[k, at, :])
            for i in range(ch):
                p = [rows[r, i * per + s * tile:i * per + (s + 1) * tile, :] for s in range(segs)]
                at = pl.multiple_of(((r * ch + i) * ch + j) * tile, tile)
                cross[pl.ds(at, sub), :] = total([a * b for a, b in zip(p, q)])
                cross[pl.ds(at + sub, sub), :] = total([a * b for a, b in zip(p, t)])
            return carry
        lax.fori_loop(0, ch, one_col, 0, unroll=4)

    def expand(r):
        mine = rows[r, body_rows:body_rows + META, :].astype(jnp.float32)
        wide = jnp.concatenate(
            [jnp.broadcast_to(mine[i:i + 1], (ch, LANES)) for i in range(ch)], axis=0)
        meta[pl.ds(pl.multiple_of(r * ch * ch, ch * ch), ch * ch), :] = wide

    def finish(k):
        raw = jnp.zeros((pairs, LAGS), jnp.float32)
        for at in range(0, tile, 2):
            left = jnp.concatenate(
                [cross[pl.ds(at + d, pairs, stride=tile), :].astype(jnp.bfloat16) for d in range(2)], axis=1)
            raw = raw + jnp.dot(left, table[at * LANES:(at + 2) * LANES, :], preferred_element_type=jnp.float32)
        theirs = cols[k, body_rows:body_rows + META, :].astype(jnp.float32)[:ch]
        theirs = jnp.concatenate([theirs] * (n_mem * ch), axis=0)
        mine = meta[...]
        count = jnp.sum(theirs * mine * seg_lane, axis=1, keepdims=True)
        dist = jnp.abs(jnp.sum((theirs - mine) * pos_lane, axis=1, keepdims=True))
        span = 1.0 + dist * ratio
        span2 = span * span
        factor = span2 / ((span2 + lag2) * (scale * jnp.maximum(count, 1.0)))
        out = (raw * factor).reshape(n_mem, ch, ch, LAGS).astype(jnp.bfloat16)
        source = flip(g, k, n_grp)
        for r in range(n_mem):
            start = flip(m, r, n_mem) * ch
            for i in range(ch):
                out_ref[start + i, source] = out[r, i]

    def first(r, carry):
        @pl.when(r > 0)
        def _():
            row_copy(r, 0, r).wait_recv()

        @pl.when((r > 1) & (r % 2 == 0))
        def _():
            row_copy(r + 1, r, 1).start()

        expand(r)
        block(r, 0)
        return carry

    lax.fori_loop(0, n_mem, first, 0)
    table_copy.wait()
    finish(0)

    def later(k, carry):
        col_copy(k).wait_recv()

        def prepare(t, c2):
            turn(k, t, cols[k, pl.ds(pl.multiple_of(t * tile, tile), tile), :].astype(jnp.float32))
            return c2

        def rest(r, c2):
            block(r, k)
            return c2

        lax.fori_loop(0, ch * segs, prepare, 0, unroll=8)
        lax.fori_loop(0, n_mem, rest, 0)
        finish(k)
        return carry

    lax.fori_loop(1, n_grp, later, 0)

    for r in range(1, n_mem):
        row_copy(r, 0, r).wait_send()
    for k in range(1, n_grp):
        col_copy(k).wait_send()


def body(spectra, seg_mask, chan_pos):
    ch, segs, _, bins = spectra.shape
    n_grp, n_mem = lax.axis_size("grp"), lax.axis_size("mem")
    flat = spectra.reshape(-1, LANES)
    size = flat.shape[0] + META
    out = pl.pallas_call(
        functools.partial(kernel, n_grp, n_mem, ch, segs, bins, LAGS / (ch * n_grp * n_mem), math.sqrt(bins)),
        out_shape=jax.ShapeDtypeStruct((n_mem * ch, n_grp, ch, LAGS), jnp.bfloat16),
        in_specs=[
            pl.BlockSpec(memory_space=pltpu.VMEM),
            pl.BlockSpec(memory_space=pltpu.SMEM),
            pl.BlockSpec(memory_space=pltpu.SMEM),
            pl.BlockSpec(memory_space=pl.ANY),
        ],
        out_specs=pl.BlockSpec(memory_space=pltpu.VMEM),
        scratch_shapes=[
            pltpu.VMEM((n_mem, size, LANES), jnp.bfloat16),
            pltpu.VMEM((n_grp, size, LANES), jnp.bfloat16),
            pltpu.VMEM((n_grp, size, LANES), jnp.bfloat16),
            pltpu.VMEM((n_mem * ch * ch, LANES), jnp.float32),
            pltpu.VMEM((n_mem * ch * ch * 2 * (bins // LANES), LANES), jnp.float32),
            pltpu.VMEM((2 * bins, LAGS), jnp.bfloat16),
            pltpu.SemaphoreType.DMA((n_mem,)),
            pltpu.SemaphoreType.DMA((n_mem,)),
            pltpu.SemaphoreType.DMA((n_grp,)),
            pltpu.SemaphoreType.DMA((n_grp,)),
            pltpu.SemaphoreType.DMA,
        ],
        compiler_params=pltpu.CompilerParams(
            collective_id=0, has_side_effects=True, vmem_limit_bytes=48 * 1024 * 1024),
    )(flat, seg_mask, chan_pos, jnp.asarray(make_table(bins, LAGS)))
    return out


def solution(mesh):
    in_specs = (P(("grp", "mem"), None, None, None), P(("grp", "mem"), None), P(("grp", "mem")))
    out_specs = P("grp", None, "mem", None)
    return jax.shard_map(body, mesh=mesh, in_specs=in_specs, out_specs=out_specs, check_vma=False)
```

time: 29.5 us -> 24.7 us (0.84)
  the two profiles are of different devices: /device:TPU:0 before, /device:TPU:1 now
where the time goes in v2:
time: 24.7 us; the launch traced here: 24.5 us
  Pallas kernels  21.7 us (88%)
  local copies, waits for them, and re-layouts  2.72 us (11%)
    pallas_call x1, Pallas kernels, body(): pl.pallas_call(functools.partial(kernel, n_grp, n_mem, ch, segs, bins, LA...  21.7 us
    unnamed x7, local copies, waits for them, and re-layouts  1.7 us
    reshape x1, local copies, waits for them, and re-layouts, body(): flat = spectra.reshape(-1, LANES)  1.02 us

profile of v2, /device:TPU:1, one launch (start us, length us, event | category | flops | bytes accessed | tf_op | source)
XLA Modules:
  0.0 24.5 jit_solution(12831405586840396384)
XLA Ops:
  0.0 0.0 copy-start.2
  0.0 0.0 copy-start.1
  0.0 1.0 %reshape.3.x_ref = bf16[512,128]{1,0:T(8,128)(2,1)S(1)} reshape(bf16[4,8,2,1024]{3,2,1,0:T(2,128)(2,1)} %param.4) | data formatting | bytes 262144 | tf_op jit(solution)/shard_map/reshape | solution.py:203
  1.0 0.0 copy-done.2
  1.0 0.0 copy-done.1
  1.0 0.0 copy-start
  1.1 1.0 %copy-done = bf16[2048,128]{1,0:T(8,128)(2,1)S(1)} copy-done((bf16[2048,128]{1,0:T(8,128)(2,1)S(1)}, bf16[2048,128]{1,0:T(8,128)(2,1)}, u32[]{:S(2)}) %copy-start) | copy-done | bytes 524312
  2.1 21.7 %shard_map.46 = bf16[32,4,4,128]{3,2,1,0:T(4,128)(2,1)S(1)} custom-call(bf16[512,128]{1,0:T(8,128)(2,1)S(1)} %reshape.3.x_ref, s32[4,8]{1,0:T(4,128)S(1)} %copy-done.1, s32[4]{0:T(128)S(1)} %copy-done.2, bf16[2048,128]{1,0:T(8,128)(2,1)S(1)} %copy-done), custom_call_target="tpu_custom_call" | custom-call | tf_op jit(solution)/shard_map/pallas_call | solution.py:205
  23.8 0.7 %copy.6 = bf16[32,4,4,128]{3,2,1,0:T(4,128)(2,1)} copy(bf16[32,4,4,128]{3,2,1,0:T(4,128)(2,1)S(1)} %shard_map.46) | data formatting | bytes 262144
Async XLA Ops:
  0.0 1.0 %copy-start.2 = (s32[4]{0:T(128)S(1)}, s32[4]{0:T(128)}, u32[]{:S(2)}) copy-start(s32[4]{0:T(128)} %pos_ref.1) | copy-start | bytes 52
  0.0 1.0 %copy-start.1 = (s32[4,8]{1,0:T(4,128)S(1)}, s32[4,8]{1,0:T(4,128)}, u32[]{:S(2)}) copy-start(s32[4,8]{1,0:T(4,128)} %mask_ref.1) | copy-start | bytes 388
  1.0 1.0 %copy-start = (bf16[2048,128]{1,0:T(8,128)(2,1)S(1)}, bf16[2048,128]{1,0:T(8,128)(2,1)}, u32[]{:S(2)}) copy-start(bf16[2048,128]{1,0:T(8,128)(2,1)} %constant.2.clone.table_hbm) | copy-start | bytes 1572868

commit v3 on v2

--- a/solution.py
+++ b/solution.py
@@ -89,8 +89,22 @@
             src_ref=rows.at[0], dst_ref=cols.at[k], send_sem=col_send.at[k], recv_sem=col_recv.at[k],
             device_id=(flip(g, k, n_grp), m), device_id_type=MESH)
 
-    for k in range(1, n_grp):
-        col_copy(k).start()
+    relay = n_grp == 4
+    middle = (g > 0) & (g < n_grp - 1)
+    passed = pltpu.make_async_remote_copy(
+        src_ref=cols.at[n_grp // 2], dst_ref=cols.at[n_grp - 1], send_sem=col_send.at[0],
+        recv_sem=col_recv.at[n_grp - 1], device_id=(flip(g, 1, n_grp), m), device_id_type=MESH)
+
+    if relay:
+        col_copy(2).start()
+        col_copy(1).start()
+
+        @pl.when(middle)
+        def _():
+            col_copy(3).start()
+    else:
+        for k in range(1, n_grp):
+            col_copy(k).start()
     for r in partners[1:]:
         row_copy(r, 0, r).start()
     row_copy(1, 0, 1).start()
@@ -113,7 +127,7 @@
             acc = acc + one
         return acc[:sub] + acc[sub:]
 
-    def block(r, k):
+    def block(r, k, slot):
         def one_col(j, carry):
             base = j * per
             q, t = [], []
@@ -123,7 +137,7 @@
                 t.append(turned[k, at, :])
             for i in range(ch):
                 p = [rows[r, i * per + s * tile:i * per + (s + 1) * tile, :] for s in range(segs)]
-                at = pl.multiple_of(((r * ch + i) * ch + j) * tile, tile)
+                at = pl.multiple_of((((slot * n_mem + r) * ch + i) * ch + j) * tile, tile)
                 cross[pl.ds(at, sub), :] = total([a * b for a, b in zip(p, q)])
                 cross[pl.ds(at + sub, sub), :] = total([a * b for a, b in zip(p, t)])
             return carry
@@ -135,11 +149,11 @@
             [jnp.broadcast_to(mine[i:i + 1], (ch, LANES)) for i in range(ch)], axis=0)
         meta[pl.ds(pl.multiple_of(r * ch * ch, ch * ch), ch * ch), :] = wide
 
-    def finish(k):
+    def finish(k, slot):
         raw = jnp.zeros((pairs, LAGS), jnp.float32)
         for at in range(0, tile, 2):
             left = jnp.concatenate(
-                [cross[pl.ds(at + d, pairs, stride=tile), :].astype(jnp.bfloat16) for d in range(2)], axis=1)
+                [cross[pl.ds(slot * pairs * tile + at + d, pairs, stride=tile), :].astype(jnp.bfloat16) for d in range(2)], axis=1)
             raw = raw + jnp.dot(left, table[at * LANES:(at + 2) * LANES, :], preferred_element_type=jnp.float32)
         theirs = cols[k, body_rows:body_rows + META, :].astype(jnp.float32)[:ch]
         theirs = jnp.concatenate([theirs] * (n_mem * ch), axis=0)
@@ -156,45 +170,93 @@
             for i in range(ch):
                 out_ref[start + i, source] = out[r, i]
 
-    def first(r, carry):
-        @pl.when(r > 0)
-        def _():
-            row_copy(r, 0, r).wait_recv()
-
-        @pl.when((r > 1) & (r % 2 == 0))
+    def prepare(k):
+        def one(t, carry):
+            turn(k, t, cols[k, pl.ds(pl.multiple_of(t * tile, tile), tile), :].astype(jnp.float32))
+            return carry
+
+        lax.fori_loop(0, ch * segs, one, 0, unroll=8)
+
+    def blocks(low, high, k, slot):
+        def one(r, carry):
+            block(r, k, slot)
+            return carry
+
+        lax.fori_loop(low, high, one, 0)
+
+    expand(0)
+    row_copy(1, 0, 1).wait_recv()
+    expand(1)
+    blocks(0, 2, 0, 0)
+    col_copy(1).wait_recv()
+    prepare(1)
+    blocks(0, 2, 1, 1)
+    table_copy.wait()
+    half = n_mem // 2 - 1
+
+    def hand_on():
+        col_copy(2).wait_recv()
+
+        @pl.when(middle)
+        def _():
+            passed.start()
+
+    def arrive(e, carry):
+        if relay:
+            @pl.when(e == min(2, half))
+            def _():
+                hand_on()
+
+        r = 2 + 2 * (e % half) + e // half
+        row_copy(r, 0, r).wait_recv()
+
+        @pl.when(e < half)
         def _():
             row_copy(r + 1, r, 1).start()
 
         expand(r)
-        block(r, 0)
+
+        def near(k, c2):
+            block(r, k, k)
+            return c2
+
+        lax.fori_loop(0, 2, near, 0)
         return carry
 
-    lax.fori_loop(0, n_mem, first, 0)
-    table_copy.wait()
-    finish(0)
+    if half:
+        lax.fori_loop(0, 2 * half, arrive, 0)
+    elif relay:
+        hand_on()
+    finish(0, 0)
+    finish(1, 1)
 
     def later(k, carry):
-        col_copy(k).wait_recv()
-
-        def prepare(t, c2):
-            turn(k, t, cols[k, pl.ds(pl.multiple_of(t * tile, tile), tile), :].astype(jnp.float32))
-            return c2
-
-        def rest(r, c2):
-            block(r, k)
-            return c2
-
-        lax.fori_loop(0, ch * segs, prepare, 0, unroll=8)
-        lax.fori_loop(0, n_mem, rest, 0)
-        finish(k)
+        if relay:
+            @pl.when(k > 2)
+            def _():
+                col_copy(k).wait_recv()
+        else:
+            col_copy(k).wait_recv()
+        prepare(k)
+        blocks(0, n_mem, k, 0)
+        finish(k, 0)
         return carry
 
-    lax.fori_loop(1, n_grp, later, 0)
+    lax.fori_loop(2, n_grp, later, 0)
 
     for r in range(1, n_mem):
         row_copy(r, 0, r).wait_send()
-    for k in range(1, n_grp):
-        col_copy(k).wait_send()
+    if relay:
+        col_copy(1).wait_send()
+        col_copy(2).wait_send()
+
+        @pl.when(middle)
+        def _():
+            col_copy(3).wait_send()
+            passed.wait_send()
+    else:
+        for k in range(1, n_grp):
+            col_copy(k).wait_send()
 
 
 def body(spectra, seg_mask, chan_pos):
@@ -209,7 +271,7 @@
             pl.BlockSpec(memory_space=pltpu.VMEM),
             pl.BlockSpec(memory_space=pltpu.SMEM),
             pl.BlockSpec(memory_space=pltpu.SMEM),
-            pl.BlockSpec(memory_space=pl.ANY),
+            pl.BlockSpec(memory_space=pltpu.HBM),
         ],
         out_specs=pl.BlockSpec(memory_space=pltpu.VMEM),
         scratch_shapes=[
@@ -217,7 +279,7 @@
             pltpu.VMEM((n_grp, size, LANES), jnp.bfloat16),
             pltpu.VMEM((n_grp, size, LANES), jnp.bfloat16),
             pltpu.VMEM((n_mem * ch * ch, LANES), jnp.float32),
-            pltpu.VMEM((n_mem * ch * ch * 2 * (bins // LANES), LANES), jnp.float32),
+            pltpu.VMEM((2 * n_mem * ch * ch * 2 * (bins // LANES), LANES), jnp.float32),
             pltpu.VMEM((2 * bins, LAGS), jnp.bfloat16),
             pltpu.SemaphoreType.DMA((n_mem,)),
             pltpu.SemaphoreType.DMA((n_mem,)),

time: 24.7 us -> 23.5 us (0.951)
  the two profiles are of different devices: /device:TPU:1 before, /device:TPU:0 now
where the time goes in v3:
time: 23.5 us; the launch traced here: 23.4 us
  Pallas kernels  20.6 us (88%)
  local copies, waits for them, and re-layouts  2.72 us (12%)
    pallas_call x1, Pallas kernels, body(): pl.pallas_call(functools.partial(kernel, n_grp, n_mem, ch, segs, bins, LA...  20.6 us
    unnamed x7, local copies, waits for them, and re-layouts  1.7 us
    reshape x1, local copies, waits for them, and re-layouts, body(): flat = spectra.reshape(-1, LANES)  1.02 us

profile of v3, /device:TPU:0, one launch (start us, length us, event | category | flops | bytes accessed | tf_op | source)
XLA Modules:
  0.0 23.4 jit_solution(18149619943981103993)
XLA Ops:
  0.0 0.0 copy-start.2
  0.0 0.0 copy-start.1
  0.0 1.0 %reshape.3.x_ref = bf16[512,128]{1,0:T(8,128)(2,1)S(1)} reshape(bf16[4,8,2,1024]{3,2,1,0:T(2,128)(2,1)} %param.4) | data formatting | bytes 262144 | tf_op jit(solution)/shard_map/reshape | solution.py:265
  1.0 0.0 copy-done.2
  1.0 0.0 copy-done.1
  1.0 0.0 copy-start
  1.1 1.0 %copy-done = bf16[2048,128]{1,0:T(8,128)(2,1)S(1)} copy-done((bf16[2048,128]{1,0:T(8,128)(2,1)S(1)}, bf16[2048,128]{1,0:T(8,128)(2,1)}, u32[]{:S(2)}) %copy-start) | copy-done | bytes 524312
  2.1 20.6 %shard_map.46 = bf16[32,4,4,128]{3,2,1,0:T(4,128)(2,1)S(1)} custom-call(bf16[512,128]{1,0:T(8,128)(2,1)S(1)} %reshape.3.x_ref, s32[4,8]{1,0:T(4,128)S(1)} %copy-done.1, s32[4]{0:T(128)S(1)} %copy-done.2, bf16[2048,128]{1,0:T(8,128)(2,1)S(1)} %copy-done), custom_call_target="tpu_custom_call" | custom-call | tf_op jit(solution)/shard_map/pallas_call | solution.py:267
  22.7 0.7 %copy.6 = bf16[32,4,4,128]{3,2,1,0:T(4,128)(2,1)} copy(bf16[32,4,4,128]{3,2,1,0:T(4,128)(2,1)S(1)} %shard_map.46) | data formatting | bytes 262144
Async XLA Ops:
  0.0 1.0 %copy-start.2 = (s32[4]{0:T(128)S(1)}, s32[4]{0:T(128)}, u32[]{:S(2)}) copy-start(s32[4]{0:T(128)} %pos_ref.1) | copy-start | bytes 52
  0.0 1.0 %copy-start.1 = (s32[4,8]{1,0:T(4,128)S(1)}, s32[4,8]{1,0:T(4,128)}, u32[]{:S(2)}) copy-start(s32[4,8]{1,0:T(4,128)} %mask_ref.1) | copy-start | bytes 388
  1.0 1.0 %copy-start = (bf16[2048,128]{1,0:T(8,128)(2,1)S(1)}, bf16[2048,128]{1,0:T(8,128)(2,1)}, u32[]{:S(2)}) copy-start(bf16[2048,128]{1,0:T(8,128)(2,1)} %constant.2.clone.table_hbm) | copy-start | bytes 1572868

commit v4 on v3

--- a/solution.py
+++ b/solution.py
@@ -288,7 +288,7 @@
             pltpu.SemaphoreType.DMA,
         ],
         compiler_params=pltpu.CompilerParams(
-            collective_id=0, has_side_effects=True, vmem_limit_bytes=48 * 1024 * 1024),
+            collective_id=0, has_side_effects=True, vmem_limit_bytes=54528 * 1024),
     )(flat, seg_mask, chan_pos, jnp.asarray(make_table(bins, LAGS)))
     return out
 

time: 23.5 us -> 22.5 us (0.957)
  local copies, waits for them, and re-layouts: 2.72 us -> 1.68 us
    unnamed x7 -> x5, local copies, waits for them, and re-layouts: 1.7 us -> 0.67 us
where the time goes in v4:
time: 22.5 us; the launch traced here: 22.3 us
  Pallas kernels  20.6 us (92%)
  local copies, waits for them, and re-layouts  1.68 us (7%)
    pallas_call x1, Pallas kernels, body(): pl.pallas_call(functools.partial(kernel, n_grp, n_mem, ch, segs, bins, LA...  20.6 us
    reshape x1, local copies, waits for them, and re-layouts, body(): flat = spectra.reshape(-1, LANES)  1.02 us
    unnamed x5, local copies, waits for them, and re-layouts  0.67 us

profile of v4, /device:TPU:0, one launch (start us, length us, event | category | flops | bytes accessed | tf_op | source)
XLA Modules:
  0.0 22.3 jit_solution(12474562529334355789)
XLA Ops:
  0.0 0.0 copy-start.1
  0.0 0.0 copy-start
  0.0 1.0 %reshape.3.x_ref = bf16[512,128]{1,0:T(8,128)(2,1)S(1)} reshape(bf16[4,8,2,1024]{3,2,1,0:T(2,128)(2,1)} %param.4) | data formatting | bytes 262144 | tf_op jit(solution)/shard_map/reshape | solution.py:265
  1.0 0.0 copy-done.1
  1.0 0.0 copy-done
  1.0 20.6 %shard_map.46 = bf16[32,4,4,128]{3,2,1,0:T(4,128)(2,1)S(1)} custom-call(bf16[512,128]{1,0:T(8,128)(2,1)S(1)} %reshape.3.x_ref, s32[4,8]{1,0:T(4,128)S(1)} %copy-done, s32[4]{0:T(128)S(1)} %copy-done.1, bf16[2048,128]{1,0:T(8,128)(2,1)} %constant.2.clone.table_hbm), custom_call_target="tpu_custom_call" | custom-call | tf_op jit(solution)/shard_map/pallas_call | solution.py:267
  21.7 0.7 %copy.6 = bf16[32,4,4,128]{3,2,1,0:T(4,128)(2,1)} copy(bf16[32,4,4,128]{3,2,1,0:T(4,128)(2,1)S(1)} %shard_map.46) | data formatting | bytes 262144
Async XLA Ops:
  0.0 1.0 %copy-start.1 = (s32[4]{0:T(128)S(1)}, s32[4]{0:T(128)}, u32[]{:S(2)}) copy-start(s32[4]{0:T(128)} %pos_ref.1) | copy-start | bytes 52
  0.0 1.0 %copy-start = (s32[4,8]{1,0:T(4,128)S(1)}, s32[4,8]{1,0:T(4,128)}, u32[]{:S(2)}) copy-start(s32[4,8]{1,0:T(4,128)} %mask_ref.1) | copy-start | bytes 388
